TPU v7x, 256 devices: a whole 4x4x8 slice. The times are simulated.
256 devices in a mesh: space: 32 (over y, x, core), frame: 8 (over z).
Axes of the slice: x: 4, y: 4, z: 8, core: 2. Of those that a mesh axis runs over, the one named last changes fastest.
Arguments:
- features: bfloat16 [8, 128, 8, 8, 512], P('frame', 'space'), may hold values from -6 to 6
- occupancy: int32 [8, 128, 512], P('frame', 'space'), may hold values 0 or 1
- w_spatial: bfloat16 [2, 27, 64, 64], replicated, may hold values from -0.21875 to 0.21875
- b_spatial: float32 [2, 64], replicated, may hold values from -3 to 3
- w_temporal: bfloat16 [3, 64, 64], replicated, may hold values from -0.75 to 0.75
- face_send: int32 [8, 64], P('frame', 'space'), may hold values from -1 to 19, as said below
- face_source: int32 [8, 128, 6], P('frame', 'space'), may hold values from -1 to 25, as said below
- send_ahead: int32 [8, 96], P('frame', 'space'), may hold values from 0 to 3, as said below
- from_prior: int32 [8, 128], P('frame', 'space'), may hold values from -1 to 2, as said below
- send_back: int32 [8, 96], P('frame', 'space'), may hold values from 0 to 3, as said below
- from_later: int32 [8, 128], P('frame', 'space'), may hold values from -1 to 2, as said below
Outputs:
- section_out: bfloat16 [8, 128, 8, 8, 512], P('frame', 'space')
Inputs may be any that keep to these rules, and one draw needn't show every extreme that they name: `face_send`: entries 0 to 0 of a device's row are the faces it sends to the device one lower in space, as brick * 6 + 0 of 1 distinct own bricks; entries 1 to 1 those it sends to the device one higher, as brick * 6 + 1 of 1 distinct own bricks; all -1 toward a side where the axis ends. `face_source`: entry (b, f) names an entry of the device's table: k < 1 a face from the device below (only for f = 0), 1 + k one from the device above (only for f = 1), 2 + 6 j + g face g of brick j of the same device, the opposite of f; or -1. Every received face is named exactly once; local pairs are mutual. `send_ahead`: each device's 3 entries are distinct bricks of that device. `from_prior`: -1 for every brick of frame 0; in other frames exactly 3 bricks of each device name a slot, each slot once. `send_back`: each device's 3 entries are distinct bricks of that device. `from_later`: -1 for every brick of the last frame; in other frames exactly 3 bricks of each device name a slot, each slot once.
All inputs are finite; a program needn't handle non-finite values. No bound on the sum of `occupancy` on one device may be relied on, other than what follows from the above.
Results may differ from a plain program's by a relative error of at most 0.0049.
Values may be sent and summed in bfloat16 or wider, within the bound.
A program may use at most 64 MiB of HBM per device.

v0:
```python
import jax
import jax.numpy as jnp
from jax import lax
from jax.sharding import PartitionSpec as P


def passed_along(x, axis, by):
    length = lax.axis_size(axis)
    pairs = [(i, i + by) for i in range(length) if 0 <= i + by < length]
    return lax.ppermute(x, axis, pairs)


def voxel_mask(occupied, edge_len, channels):
    bricks = occupied.shape[0]
    shaped = occupied.astype(jnp.float32).reshape(bricks, edge_len, edge_len, edge_len, 1)
    return jnp.broadcast_to(shaped, (bricks, edge_len, edge_len, edge_len, channels)).reshape(
        bricks, edge_len, edge_len, edge_len * channels
    )


def face_layers(field_data, edge_len, channels):
    bricks = field_data.shape[0]
    volume = field_data.reshape(bricks, edge_len, edge_len, edge_len, channels)
    planes = [
        volume[:, :, :, 0],
        volume[:, :, :, edge_len - 1],
        volume[:, :, 0],
        volume[:, :, edge_len - 1],
        volume[:, 0],
        volume[:, edge_len - 1],
    ]
    stacked = jnp.stack(
        [single.reshape(bricks, edge_len, edge_len * channels) for single in planes], axis=1
    )
    return stacked.reshape(bricks * 6, edge_len, edge_len * channels)


def padded_block(field_data, rim_faces, edge_len, channels):
    bricks = field_data.shape[0]
    wide_cols = (edge_len + 2) * channels
    inner = slice(1, edge_len + 1)
    middle = slice(channels, (edge_len + 1) * channels)
    padded = jnp.zeros((bricks, edge_len + 2, edge_len + 2, wide_cols), jnp.bfloat16)
    padded = padded.at[:, inner, inner, middle].set(field_data)
    padded = padded.at[:, inner, inner, 0:channels].set(
        rim_faces[:, 0].reshape(bricks, edge_len, edge_len, channels)
    )
    padded = padded.at[:, inner, inner, (edge_len + 1) * channels : wide_cols].set(
        rim_faces[:, 1].reshape(bricks, edge_len, edge_len, channels)
    )
    padded = padded.at[:, inner, 0, middle].set(rim_faces[:, 2])
    padded = padded.at[:, inner, edge_len + 1, middle].set(rim_faces[:, 3])
    padded = padded.at[:, 0, inner, middle].set(rim_faces[:, 4])
    padded = padded.at[:, edge_len + 1, inner, middle].set(rim_faces[:, 5])
    return padded


def conv_layer(padded, weights, bias_row, keep_mask, edge_len, channels, group_size):
    bricks = padded.shape[0]

    def one_group(pieces):
        piece_block, piece_mask = pieces
        shifted = []
        for depth_off in range(3):
            for row_off in range(3):
                for col_off in range(3):
                    shifted.append(
                        piece_block[
                            :,
                            depth_off : depth_off + edge_len,
                            row_off : row_off + edge_len,
                            col_off * channels : col_off * channels + edge_len * channels,
                        ]
                    )
        columns = jnp.stack(shifted, axis=1).reshape(
            group_size, 27, edge_len, edge_len, edge_len, channels
        )
        summed = jnp.einsum(
            "btzyxc,tcd->bzyxd", columns, weights, preferred_element_type=jnp.float32
        )
        summed = summed.reshape(group_size, edge_len, edge_len, edge_len * channels) + jnp.tile(
            bias_row, edge_len
        )
        return (jnp.maximum(summed, 0.0) * piece_mask).astype(jnp.bfloat16)

    grouped = lax.map(
        one_group,
        (
            padded.reshape((bricks // group_size, group_size) + padded.shape[1:]),
            keep_mask.reshape((bricks // group_size, group_size) + keep_mask.shape[1:]),
        ),
    )
    return grouped.reshape(bricks, edge_len, edge_len, edge_len * channels)


def per_device(
    features,
    occupancy,
    w_spatial,
    b_spatial,
    w_temporal,
    face_send,
    face_source,
    send_ahead,
    from_prior,
    send_back,
    from_later,
):
    channels = w_spatial.shape[-1]
    edge_len = features.shape[2]
    bricks = features.shape[1]
    layers = w_spatial.shape[0]
    slab_count = face_send.shape[1] // 2
    keep_mask = voxel_mask(occupancy[0], edge_len, channels)
    inputs = (features[0].astype(jnp.float32) * keep_mask).astype(jnp.bfloat16)
    sources = face_source[0]
    outgoing = face_send[0]
    hidden = inputs
    for layer_index in range(layers):
        face_table = face_layers(hidden, edge_len, channels)
        outbound = jnp.where((outgoing >= 0)[:, None, None], face_table[jnp.clip(outgoing, 0)], 0)
        parcels = outbound.reshape(2, slab_count, edge_len, edge_len * channels)
        below_faces = passed_along(parcels[1], "space", 1)
        above_faces = passed_along(parcels[0], "space", -1)
        arrived = jnp.concatenate([below_faces, above_faces], axis=0)
        table = jnp.concatenate([arrived, face_table], axis=0)
        rim_faces = jnp.where((sources >= 0)[:, :, None, None], table[jnp.clip(sources, 0)], 0)
        padded = padded_block(hidden, rim_faces, edge_len, channels)
        hidden = conv_layer(
            padded, w_spatial[layer_index], b_spatial[layer_index], keep_mask, edge_len, channels, 2
        )
    ahead_rows = hidden[send_ahead[0]]
    prior_rows = passed_along(ahead_rows, "frame", 1)
    back_rows = hidden[send_back[0]]
    later_rows = passed_along(back_rows, "frame", -1)
    prior_slots = from_prior[0]
    later_slots = from_later[0]
    from_before = jnp.where(
        (prior_slots >= 0)[:, None, None, None], prior_rows[jnp.clip(prior_slots, 0)], 0
    )
    from_after = jnp.where(
        (later_slots >= 0)[:, None, None, None], later_rows[jnp.clip(later_slots, 0)], 0
    )
    temporal_sum = jnp.dot(
        from_before.reshape(-1, channels), w_temporal[0], preferred_element_type=jnp.float32
    )
    temporal_sum = temporal_sum + jnp.dot(
        hidden.reshape(-1, channels), w_temporal[1], preferred_element_type=jnp.float32
    )
    temporal_sum = temporal_sum + jnp.dot(
        from_after.reshape(-1, channels), w_temporal[2], preferred_element_type=jnp.float32
    )
    total_sum = inputs.astype(jnp.float32) + temporal_sum.reshape(
        bricks, edge_len, edge_len, edge_len * channels
    )
    return (keep_mask * total_sum).astype(jnp.bfloat16)[None]


def solution(mesh):
    in_specs = (
        P("frame", "space", None, None, None),
        P("frame", "space", None),
        P(),
        P(),
        P(),
        P("frame", "space"),
        P("frame", "space", None),
        P("frame", "space"),
        P("frame", "space"),
        P("frame", "space"),
        P("frame", "space"),
    )
    out_specs = P("frame", "space", None, None, None)
    return jax.shard_map(
        per_device, mesh=mesh, in_specs=in_specs, out_specs=out_specs, check_vma=False
    )
```

profile of v0, /device:TPU:120, one launch (start us, length us, event | category | flops | bytes accessed | tf_op | source)
XLA Modules:
  0.0 300.4 jit_solution(10833556042566975725)
XLA Ops:
  0.9 1.2 reshape.908
  5.9 4.3 %collective-permute-start.1 = (bf16[1,8,512]{2,1,0:T(8,128)(2,1)S(1)}, bf16[1,8,512]{2,1,0:T(8,128)(2,1)S(1)}, u32[]{:S(2)}, u32[]{:S(2)}) collective-permute-start(bf16[1,8,512]{2,1,0:T(8,128)(2,1)S(1)} %get-tuple-element.346), channel_id=1, source_target_pairs={{8,0},{16,8},{24,16},{32,24},{40,32},{48,40},{56,48},{64,56},{72,6... | collective-permute-start | bytes 24584 | tf_op jit(solution)/shard_map/ppermute | solution.py:10
  10.1 1.9 collective-permute-start
  14.1 1.2 compare_bitcast_fusion
  15.3 1.2 maximum_bitcast_fusion.1
  16.5 1.2 compare_bitcast_fusion.3
  18.5 1.2 slice_bitcast_fusion
  20.1 1.4 scatter.46
  22.5 3.5 %scatter.49 = bf16[4,10,10,640]{3,2,1,0:T(8,128)(2,1)} dynamic-update-slice(bf16[4,10,10,640]{3,2,1,0:T(8,128)(2,1)} %scatter.46, bf16[4,8,8,64]{3,2,1,0:T(8,128)(2,1)S(1)} %reshape.893, s32[]{:T(128)} %copy.143, s32[]{:T(128)} %constant.417.clone.1, s32[]{:T(128)} %constant.417.clone.1, s32[]{:T(128)} %copy.143) | dynamic-update-slice | bytes 65540 | tf_op jit(solution)/shard_map/scatter | solution.py:45
  26.1 10.5 %scatter.50 = bf16[4,10,10,640]{3,2,1,0:T(8,128)(2,1)} dynamic-update-slice(bf16[4,10,10,640]{3,2,1,0:T(8,128)(2,1)} %scatter.49, bf16[4,8,8,64]{3,2,1,0:T(8,128)(2,1)S(1)} %reshape.894, s32[]{:T(128)} %copy.143, s32[]{:T(128)} %constant.417.clone.1, s32[]{:T(128)} %constant.417.clone.1, s32[]{:T(128)} %constant.418.clone.1) | dynamic-update-slice | bytes 65540 | tf_op jit(solution)/shard_map/scatter | solution.py:48
  36.5 7.9 %scatter.51 = bf16[4,10,10,640]{3,2,1,0:T(8,128)(2,1)} dynamic-update-slice(bf16[4,10,10,640]{3,2,1,0:T(8,128)(2,1)} %scatter.50, bf16[4,8,1,512]{3,2,1,0:T(2,128)(2,1)S(1)} %copy.25, s32[]{:T(128)} %copy.143, s32[]{:T(128)} %constant.417.clone.1, s32[]{:T(128)} %copy.143, s32[]{:T(128)} %constant.419.clone.1) | dynamic-update-slice | bytes 65540 | tf_op jit(solution)/shard_map/scatter | solution.py:51
  44.4 7.8 %scatter.54 = bf16[4,10,10,640]{3,2,1,0:T(8,128)(2,1)} dynamic-update-slice(bf16[4,10,10,640]{3,2,1,0:T(8,128)(2,1)} %scatter.51, bf16[4,8,1,512]{3,2,1,0:T(2,128)(2,1)S(1)} %copy.26, s32[]{:T(128)} %copy.143, s32[]{:T(128)} %constant.417.clone.1, s32[]{:T(128)} %constant.420.clone.1, s32[]{:T(128)} %constant.419.clone.1) | dynamic-update-slice | bytes 65540 | tf_op jit(solution)/shard_map/scatter | solution.py:52
  52.2 3.4 %scatter.55 = bf16[4,10,10,640]{3,2,1,0:T(8,128)(2,1)} dynamic-update-slice(bf16[4,10,10,640]{3,2,1,0:T(8,128)(2,1)} %scatter.54, bf16[4,1,8,512]{3,2,1,0:T(8,128)(2,1)S(1)} %get-tuple-element.338, s32[]{:T(128)} %copy.143, s32[]{:T(128)} %copy.143, s32[]{:T(128)} %constant.417.clone.1, s32[]{:T(128)} %constant.419.clone.1) | dynamic-update-slice | bytes 65540 | tf_op jit(solution)/shard_map/scatter | solution.py:53
  55.6 3.4 %scatter.56 = bf16[4,10,10,640]{3,2,1,0:T(8,128)(2,1)} dynamic-update-slice(bf16[4,10,10,640]{3,2,1,0:T(8,128)(2,1)} %scatter.55, bf16[4,1,8,512]{3,2,1,0:T(8,128)(2,1)S(1)} %get-tuple-element.337, s32[]{:T(128)} %copy.143, s32[]{:T(128)} %constant.420.clone.1, s32[]{:T(128)} %constant.417.clone.1, s32[]{:T(128)} %constant.419.clone.1) | dynamic-update-slice | bytes 65540 | tf_op jit(solution)/shard_map/scatter | solution.py:54
  59.7 103.2 %while.34 = (s32[]{:T(128)}, bf16[2,2,8,8,512]{4,3,2,1,0:T(8,128)(2,1)}, bf16[2,2,10,10,640]{4,3,2,1,0:T(8,128)(2,1)}, bf16[27,64,64]{2,1,0:T(8,128)(2,1)S(1)}, ...) while((s32[]{:T(128)}, bf16[2,2,8,8,512]{4,3,2,1,0:T(8,128)(2,1)}, ...), condition=%wide.region_1.2_spmd, body=%wide.region_0.1_spmd.sunk | while | flops 226754560 | bytes 33116592 | solution.py:86
  63.7 1.1 stack.231
  65.5 1.1 stack.232
  67.4 1.1 stack.233
  69.3 1.1 stack.234
  74.0 1.6 fusion.47
  75.6 1.1 stack.238
  105.5 4.8 %convolution_bitcast_fusion.4 = f32[2,8,8,8,64]{4,3,2,1,0:T(8,128)S(1)} fusion(bf16[2,27,8,8,8,64]{5,4,1,3,2,0:T(8,128)(2,1)} %constant_dynamic-update-slice_fusion.146, bf16[27,64,64]{2,1,0:T(8,128)(2,1)S(1)} %get-tuple-element.550), kind=kOutput, calls=%fused_computation.8.clone.1 | convolution fusion | flops 226492416 | bytes 4022272 | tf_op jit(solution)/shard_map/while/body/eval_jaxpr/btzyxc,tcd->bzyxd/dot_general | solution.py:78
  125.6 1.6 fusion.47
  127.2 1.1 stack.238
  157.1 4.8 %convolution_bitcast_fusion.4 = f32[2,8,8,8,64]{4,3,2,1,0:T(8,128)S(1)} fusion(bf16[2,27,8,8,8,64]{5,4,1,3,2,0:T(8,128)(2,1)} %constant_dynamic-update-slice_fusion.146, bf16[27,64,64]{2,1,0:T(8,128)(2,1)S(1)} %get-tuple-element.550), kind=kOutput, calls=%fused_computation.8.clone.1 | convolution fusion | flops 226492416 | bytes 4022272 | tf_op jit(solution)/shard_map/while/body/eval_jaxpr/btzyxc,tcd->bzyxd/dot_general | solution.py:78
  162.9 1.3 reshape_reshape.11
  167.1 5.7 %collective-permute-start.3 = (bf16[1,8,512]{2,1,0:T(8,128)(2,1)S(1)}, bf16[1,8,512]{2,1,0:T(8,128)(2,1)S(1)}, u32[]{:S(2)}, u32[]{:S(2)}) collective-permute-start(bf16[1,8,512]{2,1,0:T(8,128)(2,1)S(1)} %get-tuple-element.344), channel_id=1, source_target_pairs={{8,0},{16,8},{24,16},{32,24},{40,32},{48,40},{56,48},{64,56},{72,6... | collective-permute-start | bytes 24584 | tf_op jit(solution)/shard_map/ppermute | solution.py:10
  172.9 1.9 collective-permute-start.2
  175.4 1.1 reshape.890
  176.5 1.4 scatter.59
  177.9 2.0 collective-permute-done.2
  181.0 1.4 scatter.60
  182.4 9.8 %scatter.61 = bf16[4,10,10,640]{3,2,1,0:T(8,128)(2,1)S(1)} dynamic-update-slice(bf16[4,10,10,640]{3,2,1,0:T(8,128)(2,1)S(1)} %scatter.60, bf16[4,8,8,64]{3,2,1,0:T(8,128)(2,1)S(1)} %reshape.901, s32[]{:T(128)} %copy.143, s32[]{:T(128)} %constant.417.clone.1, s32[]{:T(128)} %constant.417.clone.1, s32[]{:T(128)} %constant.418.clone.1) | dynamic-update-slice | bytes 65540 | tf_op jit(solution)/shard_map/scatter | solution.py:48
  192.2 6.5 %scatter.64 = bf16[4,10,10,640]{3,2,1,0:T(8,128)(2,1)S(1)} dynamic-update-slice(bf16[4,10,10,640]{3,2,1,0:T(8,128)(2,1)S(1)} %scatter.61, bf16[4,8,1,512]{3,2,1,0:T(2,128)(2,1)S(1)} %copy.35, s32[]{:T(128)} %copy.143, s32[]{:T(128)} %constant.417.clone.1, s32[]{:T(128)} %copy.143, s32[]{:T(128)} %constant.419.clone.1) | dynamic-update-slice | bytes 65540 | tf_op jit(solution)/shard_map/scatter | solution.py:51
  198.7 6.5 %scatter.65 = bf16[4,10,10,640]{3,2,1,0:T(8,128)(2,1)S(1)} dynamic-update-slice(bf16[4,10,10,640]{3,2,1,0:T(8,128)(2,1)S(1)} %scatter.64, bf16[4,8,1,512]{3,2,1,0:T(2,128)(2,1)S(1)} %copy.36, s32[]{:T(128)} %copy.143, s32[]{:T(128)} %constant.417.clone.1, s32[]{:T(128)} %constant.420.clone.1, s32[]{:T(128)} %constant.419.clone.1) | dynamic-update-slice | bytes 65540 | tf_op jit(solution)/shard_map/scatter | solution.py:52
  205.3 1.8 scatter.66
  207.1 1.8 scatter.69
  209.6 73.4 %while.35 = (s32[]{:T(128)}, bf16[2,2,8,8,512]{4,3,2,1,0:T(8,128)(2,1)}, bf16[2,2,10,10,640]{4,3,2,1,0:T(8,128)(2,1)S(1)}, bf16[27,64,64]{2,1,0:T(8,128)(2,1)S(1...) while((s32[]{:T(128)}, bf16[2,2,8,8,512]{4,3,2,1,0:T(8,128)(2,1)}, ...), condition=%wide.region_3.4_spmd, body=%wide.region_2.3_spmd.sunk | while | flops 226754560 | bytes 36688332 | solution.py:86
  218.5 1.2 fusion.52
  240.5 4.8 %convolution_bitcast_fusion.5 = f32[2,8,8,8,64]{4,3,2,1,0:T(8,128)S(1)} fusion(bf16[2,27,8,8,8,64]{5,4,1,3,2,0:T(8,128)(2,1)} %constant_dynamic-update-slice_fusion.173, bf16[27,64,64]{2,1,0:T(8,128)(2,1)S(1)} %get-tuple-element.571), kind=kOutput, calls=%fused_computation.40.clone.1 | convolution fusion | flops 226492416 | bytes 4022272 | tf_op jit(solution)/shard_map/while/body/eval_jaxpr/btzyxc,tcd->bzyxd/dot_general | solution.py:78
  255.2 1.2 fusion.52
  277.2 4.8 %convolution_bitcast_fusion.5 = f32[2,8,8,8,64]{4,3,2,1,0:T(8,128)S(1)} fusion(bf16[2,27,8,8,8,64]{5,4,1,3,2,0:T(8,128)(2,1)} %constant_dynamic-update-slice_fusion.173, bf16[27,64,64]{2,1,0:T(8,128)(2,1)S(1)} %get-tuple-element.571), kind=kOutput, calls=%fused_computation.40.clone.1 | convolution fusion | flops 226492416 | bytes 4022272 | tf_op jit(solution)/shard_map/while/body/eval_jaxpr/btzyxc,tcd->bzyxd/dot_general | solution.py:78
  283.0 1.3 reshape_reshape.12
  284.3 1.5 gather_fusion.6
  285.9 2.0 collective-permute-start.5
  287.9 1.5 gather_fusion.4
  289.4 5.0 %collective-permute-start.4 = (bf16[3,8,8,512]{3,2,1,0:T(8,128)(2,1)S(1)}, bf16[3,8,8,512]{3,2,1,0:T(8,128)(2,1)S(1)}, u32[]{:S(2)}, u32[]{:S(2)}) collective-permute-start(bf16[3,8,8,512]{3,2,1,0:T(8,128)(2,1)S(1)} %gather_fusion.4), channel_id=1, source_target_pairs={{0,1},{1,2},{2,3},{3,4},{4,5},{5,6},{6,7},{8,9},{9,10},{10,11},{11... | collective-permute-start | bytes 589832 | tf_op jit(solution)/shard_map/ppermute | solution.py:10
  296.1 1.5 collective-permute-done.4
  (380 shorter events, 163.1 us)
Async XLA Ops:
  0.0 18.3 %copy-start.7 = (bf16[1,4,8,8,512]{4,3,2,1,0:T(8,128)(2,1)S(1)}, bf16[1,4,8,8,512]{4,3,2,1,0:T(8,128)(2,1)}, u32[]{:S(2)}) copy-start(bf16[1,4,8,8,512]{4,3,2,1,0:T(8,128)(2,1)} %param.43) | copy-start | bytes 786436
  0.0 19.7 %copy-start.12 = (f32[2,64]{1,0:T(2,128)S(1)}, f32[2,64]{1,0:T(2,128)}, u32[]{:S(2)}) copy-start(f32[2,64]{1,0:T(2,128)} %param.46) | copy-start | bytes 1540
  0.0 19.7 %copy-start.15 = (s32[1,3]{1,0:T(1,128)S(1)}, s32[1,3]{1,0:T(1,128)}, u32[]{:S(2)}) copy-start(s32[1,3]{1,0:T(1,128)} %param.52) | copy-start | bytes 40
  0.0 19.8 %copy-start.16 = (s32[1,3]{1,0:T(1,128)S(1)}, s32[1,3]{1,0:T(1,128)}, u32[]{:S(2)}) copy-start(s32[1,3]{1,0:T(1,128)} %param.50) | copy-start | bytes 40
  4.2 15.6 %copy-start.11 = (pred[2]{0:T(512)(128)(4,1)}, pred[2]{0:T(512)(128)(4,1)S(1)}, u32[]{:S(2)}) copy-start(pred[2]{0:T(512)(128)(4,1)S(1)} %compare_bitcast_fusion.1) | copy-start | bytes 10
  5.9 15.6 %collective-permute-start.1 = (bf16[1,8,512]{2,1,0:T(8,128)(2,1)S(1)}, bf16[1,8,512]{2,1,0:T(8,128)(2,1)S(1)}, u32[]{:S(2)}, u32[]{:S(2)}) collective-permute-start(bf16[1,8,512]{2,1,0:T(8,128)(2,1)S(1)} %get-tuple-element.346), channel_id=1, source_target_pairs={{8,0},{16,8},{24,16},{32,24},{40,32},{48,40},{56,48},{64,56},{72,6... | collective-permute-start | bytes 24584 | tf_op jit(solution)/shard_map/ppermute | solution.py:10
  10.1 11.3 %collective-permute-start = (bf16[1,8,512]{2,1,0:T(8,128)(2,1)S(1)}, bf16[1,8,512]{2,1,0:T(8,128)(2,1)S(1)}, u32[]{:S(2)}, u32[]{:S(2)}) collective-permute-start(bf16[1,8,512]{2,1,0:T(8,128)(2,1)S(1)} %get-tuple-element.345), channel_id=1, source_target_pairs={{0,8},{8,16},{16,24},{24,32},{32,40},{40,48},{48,56},{56,64},{64,7... | collective-permute-start | bytes 24584 | tf_op jit(solution)/shard_map/ppermute | solution.py:10
  75.6 25.1 %copy-start = (bf16[2,8,8,512]{3,2,1,0:T(8,128)(2,1)S(1)}, bf16[2,8,8,512]{3,2,1,0:T(8,128)(2,1)}, u32[]{:S(2)}) copy-start(bf16[2,8,8,512]{3,2,1,0:T(8,128)(2,1)} %get-tuple-element.495) | copy-start | bytes 393220 | tf_op jit(solution)/shard_map/while
  101.7 8.9 %copy-start.5 = (bf16[2,2,8,8,512]{4,3,2,1,0:T(8,128)(2,1)S(1)}, bf16[2,2,8,8,512]{4,3,2,1,0:T(8,128)(2,1)}, u32[]{:S(2)}) copy-start(bf16[2,2,8,8,512]{4,3,2,1,0:T(8,128)(2,1)} %get-tuple-element.541) | copy-start | bytes 786436 | tf_op jit(solution)/shard_map/while
  110.6 0.7 copy-start.6
  127.2 25.1 %copy-start = (bf16[2,8,8,512]{3,2,1,0:T(8,128)(2,1)S(1)}, bf16[2,8,8,512]{3,2,1,0:T(8,128)(2,1)}, u32[]{:S(2)}) copy-start(bf16[2,8,8,512]{3,2,1,0:T(8,128)(2,1)} %get-tuple-element.495) | copy-start | bytes 393220 | tf_op jit(solution)/shard_map/while
  153.3 8.9 %copy-start.5 = (bf16[2,2,8,8,512]{4,3,2,1,0:T(8,128)(2,1)S(1)}, bf16[2,2,8,8,512]{4,3,2,1,0:T(8,128)(2,1)}, u32[]{:S(2)}) copy-start(bf16[2,2,8,8,512]{4,3,2,1,0:T(8,128)(2,1)} %get-tuple-element.541) | copy-start | bytes 786436 | tf_op jit(solution)/shard_map/while
  162.2 0.7 copy-start.6
  167.1 10.8 %collective-permute-start.3 = (bf16[1,8,512]{2,1,0:T(8,128)(2,1)S(1)}, bf16[1,8,512]{2,1,0:T(8,128)(2,1)S(1)}, u32[]{:S(2)}, u32[]{:S(2)}) collective-permute-start(bf16[1,8,512]{2,1,0:T(8,128)(2,1)S(1)} %get-tuple-element.344), channel_id=1, source_target_pairs={{8,0},{16,8},{24,16},{32,24},{40,32},{48,40},{56,48},{64,56},{72,6... | collective-permute-start | bytes 24584 | tf_op jit(solution)/shard_map/ppermute | solution.py:10
  172.9 7.1 %collective-permute-start.2 = (bf16[1,8,512]{2,1,0:T(8,128)(2,1)S(1)}, bf16[1,8,512]{2,1,0:T(8,128)(2,1)S(1)}, u32[]{:S(2)}, u32[]{:S(2)}) collective-permute-start(bf16[1,8,512]{2,1,0:T(8,128)(2,1)S(1)} %get-tuple-element.343), channel_id=1, source_target_pairs={{0,8},{8,16},{16,24},{24,32},{32,40},{40,48},{48,56},{56,64},{64,7... | collective-permute-start | bytes 24584 | tf_op jit(solution)/shard_map/ppermute | solution.py:10
  209.6 84.8 %copy-start.10 = (bf16[3,64,64]{2,1,0:T(8,128)(2,1)S(1)}, bf16[3,64,64]{2,1,0:T(8,128)(2,1)}, u32[]{:S(2)}) copy-start(bf16[3,64,64]{2,1,0:T(8,128)(2,1)} %param.47) | copy-start | bytes 73732
  209.6 85.8 %copy-start.14 = (pred[4]{0:T(512)(128)(4,1)S(1)}, pred[4]{0:T(512)(128)(4,1)}, u32[]{:S(2)}) copy-start(pred[4]{0:T(512)(128)(4,1)} %compare_bitcast_fusion) | copy-start | bytes 16
  209.6 88.6 %copy-start.13 = (pred[4]{0:T(512)(128)(4,1)S(1)}, pred[4]{0:T(512)(128)(4,1)}, u32[]{:S(2)}) copy-start(pred[4]{0:T(512)(128)(4,1)} %compare_bitcast_fusion.3) | copy-start | bytes 16
  209.6 0.9 copy-start.1
  235.0 10.6 %copy-start.3 = (bf16[2,2,8,8,512]{4,3,2,1,0:T(8,128)(2,1)S(1)}, bf16[2,2,8,8,512]{4,3,2,1,0:T(8,128)(2,1)}, u32[]{:S(2)}) copy-start(bf16[2,2,8,8,512]{4,3,2,1,0:T(8,128)(2,1)} %get-tuple-element.562) | copy-start | bytes 786436 | tf_op jit(solution)/shard_map/while
  235.7 10.6 %copy-start.2 = (bf16[2,2,10,10,640]{4,3,2,1,0:T(8,128)(2,1)S(1)}, bf16[2,2,10,10,640]{4,3,2,1,0:T(8,128)(2,1)}, u32[]{:S(2)}) copy-start(bf16[2,2,10,10,640]{4,3,2,1,0:T(8,128)(2,1)} %copy-done.1) | copy-start | bytes 1536004 | tf_op jit(solution)/shard_map/while
  245.6 0.7 copy-start.4
  246.3 0.9 copy-start.1
  271.6 10.6 %copy-start.3 = (bf16[2,2,8,8,512]{4,3,2,1,0:T(8,128)(2,1)S(1)}, bf16[2,2,8,8,512]{4,3,2,1,0:T(8,128)(2,1)}, u32[]{:S(2)}) copy-start(bf16[2,2,8,8,512]{4,3,2,1,0:T(8,128)(2,1)} %get-tuple-element.562) | copy-start | bytes 786436 | tf_op jit(solution)/shard_map/while
  272.4 10.6 %copy-start.2 = (bf16[2,2,10,10,640]{4,3,2,1,0:T(8,128)(2,1)S(1)}, bf16[2,2,10,10,640]{4,3,2,1,0:T(8,128)(2,1)}, u32[]{:S(2)}) copy-start(bf16[2,2,10,10,640]{4,3,2,1,0:T(8,128)(2,1)} %copy-done.1) | copy-start | bytes 1536004 | tf_op jit(solution)/shard_map/while
  282.3 0.7 copy-start.4
  283.0 16.5 %copy-start.8 = (bf16[1,4,8,8,512]{4,3,2,1,0:T(8,128)(2,1)S(1)}, bf16[1,4,8,8,512]{4,3,2,1,0:T(8,128)(2,1)}, u32[]{:S(2)}) copy-start(bf16[1,4,8,8,512]{4,3,2,1,0:T(8,128)(2,1)} %param.43) | copy-start | bytes 786436
  283.0 16.5 %copy-start.9 = (f32[1,4,8,8,512]{4,3,2,1,0:T(8,128)S(1)}, f32[1,4,8,8,512]{4,3,2,1,0:T(8,128)}, u32[]{:S(2)}) copy-start(f32[1,4,8,8,512]{4,3,2,1,0:T(8,128)} %reshape.890) | copy-start | bytes 1572868
  285.9 8.9 %collective-permute-start.5 = (bf16[3,8,8,512]{3,2,1,0:T(8,128)(2,1)S(1)}, bf16[3,8,8,512]{3,2,1,0:T(8,128)(2,1)S(1)}, u32[]{:S(2)}, u32[]{:S(2)}) collective-permute-start(bf16[3,8,8,512]{3,2,1,0:T(8,128)(2,1)S(1)} %gather_fusion.6), channel_id=1, source_target_pairs={{1,0},{2,1},{3,2},{4,3},{5,4},{6,5},{7,6},{9,8},{10,9},{11,10},{12... | collective-permute-start | bytes 589832 | tf_op jit(solution)/shard_map/ppermute | solution.py:10
  289.4 8.2 %collective-permute-start.4 = (bf16[3,8,8,512]{3,2,1,0:T(8,128)(2,1)S(1)}, bf16[3,8,8,512]{3,2,1,0:T(8,128)(2,1)S(1)}, u32[]{:S(2)}, u32[]{:S(2)}) collective-permute-start(bf16[3,8,8,512]{3,2,1,0:T(8,128)(2,1)S(1)} %gather_fusion.4), channel_id=1, source_target_pairs={{0,1},{1,2},{2,3},{3,4},{4,5},{5,6},{6,7},{8,9},{9,10},{10,11},{11... | collective-permute-start | bytes 589832 | tf_op jit(solution)/shard_map/ppermute | solution.py:10
where the time goes:
time: 303 us; the launch traced here: 300 us
  local copies, waits for them, and re-layouts  243 us (80%)
  starting transfers between devices  20.9 us (7%)
  matrix products  20.3 us (7%)
  other arithmetic  11 us (4%)
  waiting for transfers between devices  3.57 us (1%)
    while x132, local copies, waits for them, and re-layouts  83.6 us
    another operation x112, local copies, waits for them, and re-layouts, one_group(): jnp.stack(shifted, axis=1)  61.4 us
    ppermute x6, starting transfers between devices, passed_along(): return lax.ppermute(x, axis, pairs)  20.9 us
    scatter x2, local copies, waits for them, and re-layouts, padded_block(): padded.at[:, inner, inner, (edge_len + 1) * channels:wide_cols]  20.2 us
    dot_general x4, matrix products, one_group(): jnp.einsum('btzyxc,tcd->bzyxd', columns, weights, preferred_element_type=...  19.3 us
    scatter x2, local copies, waits for them, and re-layouts, padded_block(): padded = padded.at[:, inner, 0, middle].set(rim_faces[:, 2])  14.4 us
    scatter x2, local copies, waits for them, and re-layouts, padded_block(): padded = padded.at[:, inner, edge_len + 1, middle].set(rim_faces[:, 3])  14.4 us
    slice x8, local copies, waits for them, and re-layouts, one_group(): piece_block[:, depth_off:depth_off + edge_len, row_off:row_off + edge_len...  8.27 us
  transfers between devices with their start and end apart: 6, of which 2 were waited for; matrix products, arithmetic and copies ran while one was open for 5% of the time, Pallas kernels for 0%

commit v1 on v0

v1 whole, which is shorter than its diff:
```python
import jax
import jax.numpy as jnp
from jax import lax
from jax.experimental import pallas as pl
from jax.experimental.pallas import tpu as pltpu
from jax.sharding import PartitionSpec as P

MESH = pl.DeviceIdType.MESH
F32 = jnp.float32
BF16 = jnp.bfloat16
PAIRS = (1, 2, 0, 3)
INNER, OUTER = slice(0, 16), slice(16, 32)


def below(x, edge, row):
    return pltpu.roll(jnp.where(row == 7, edge, x), 1, axis=x.ndim - 2)


def above(x, edge, row):
    return pltpu.roll(jnp.where(row == 0, edge, x), 7, axis=x.ndim - 2)


def three(x, low, high, row):
    return below(x, low, row), x, above(x, high, row)


def pair(a, b):
    return jnp.concatenate([a, b], axis=-2).astype(BF16)


def put_layers(S, dy, at, rows, lanes, x):
    x = x.reshape((4, 2) + x.shape[1:])
    S[1, dy, at, 0:4, rows, lanes] = x[:, 0]
    S[0, dy, at, 1:5, rows, lanes] = x[:, 1]


def left_side(S, rows):
    pieces = []
    for zz in range(4):
        for dy in range(3):
            x = S[zz % 2, dy, :, zz // 2 : zz // 2 + 4, rows, :]
            pieces.append(x.reshape(-1, 256))
    return jnp.concatenate(pieces, axis=1)


def kernel(
    feats, occ, wsp, bsp, wtm, fsend, fsrc, sahead, fprior, sback, flater, out,
    fin, occv, wv, bv, wtv, M, H0, H1, ACC, S1, S2, SV, W, WT, VH, CR, msg, rmsg,
    sE, rE, sL, rL, H2, BASE, lsem, msend, mrecv, esend, erecv, lsend, lrecv,
):
    s, f = lax.axis_index("space"), lax.axis_index("frame")
    n_s, n_f = lax.axis_size("space"), lax.axis_size("frame")
    lo, hi, be, af = s > 0, s < n_s - 1, f > 0, f < n_f - 1

    loads = [
        pltpu.make_async_copy(src, dst, lsem.at[i])
        for i, (src, dst) in enumerate(
            ((occ.at[0], occv), (feats.at[0], fin), (wsp, wv), (bsp, bv), (wtm, wtv))
        )
    ]
    for c in loads:
        c.start()

    barrier = pltpu.get_barrier_semaphore()
    for there, to in (
        (lo, {"space": s - 1}),
        (hi, {"space": s + 1}),
        (be, {"frame": f - 1}),
        (af, {"frame": f + 1}),
    ):

        @pl.when(there)
        def _(to=to):
            pl.semaphore_signal(barrier, 1, device_id=to, device_id_type=MESH)

    lane = lax.broadcasted_iota(jnp.int32, (1, 1, 128), 2)
    left = lane < 64
    row = lax.broadcasted_iota(jnp.int32, (1, 8, 128), 1)
    row2 = lax.broadcasted_iota(jnp.int32, (8, 128), 0)

    loads[0].wait()
    voxel = lax.broadcasted_iota(jnp.int32, (64, 512), 1)
    mine = (voxel >> 3) == lax.broadcasted_iota(jnp.int32, (64, 512), 0)
    o = occv[...].astype(F32)
    spread = jnp.concatenate(
        [jnp.where(mine, o[b : b + 1, :], 0.0).astype(BF16) for b in range(4)], axis=0
    )
    r = lax.broadcasted_iota(jnp.int32, (16, 512), 0) & 7
    c = lax.broadcasted_iota(jnp.int32, (16, 512), 1) >> 6
    widen = jnp.where(r == c, 1.0, 0.0).astype(BF16)
    widen = jnp.concatenate([widen] * 32, axis=0)
    m = jnp.dot(spread, widen, preferred_element_type=F32)
    loads[1].wait()
    for g in range(4):
        mg = m[:, g * 128 : (g + 1) * 128].reshape(4, 4, 2, 8, 128)
        M[:, :, :, g] = mg
        x = fin[:, :, :, g * 128 : (g + 1) * 128].astype(F32)
        H0[:, :, :, g] = x.reshape(4, 4, 2, 8, 128) * mg

    def tile(H, b, g):
        return H[b, :, :, g].reshape(8, 8, 128)

    def rim(b, face):
        e = fsrc[0, b, face]
        return e >= 2, jnp.maximum(e - 2, 0) // 6

    def rim_tile(H, b, face, g):
        has, j = rim(b, face)
        return jnp.where(has, tile(H, j, g), 0.0)

    def rim_layer(H, b, face, g):
        has, j = rim(b, face)
        z = 7 if face == 4 else 0
        return jnp.where(has, H[j, z // 2, z % 2, g], 0.0)

    down = jnp.maximum(fsend[0, 0], 0) // 6
    up = jnp.maximum(fsend[0, 1], 0) // 6

    def rows16(x):
        return x.reshape(-1, 128).astype(BF16).reshape(-1, 16, 128)

    def parcel(k, b, g, face, other):
        beyond = rim_tile(H0, b, face, other)
        mask = tile(M, b, g)
        asked = jnp.where(fsrc[0, b, face] == face, 1.0, 0.0)
        mixed = jnp.where(left, beyond, mask) if k == 0 else jnp.where(left, mask, beyond)
        edges = jnp.where(row == 0, rim_tile(H0, b, 3, g), asked)
        edges = jnp.where(row == 7, rim_tile(H0, b, 2, g), edges)
        msg[k, 0:4] = rows16(tile(H0, b, g))
        msg[k, 4:8] = rows16(mixed)
        msg[k, 8:12] = rows16(edges)
        msg[k, 12] = pair(rim_layer(H0, b, 4, g), rim_layer(H0, b, 5, g))

    parcel(0, up, 3, 1, 0)
    parcel(1, down, 0, 0, 3)

    for k, ends in ((0, s == 0), (1, s == n_s - 1)):

        @pl.when(ends)
        def _(k=k):
            rmsg[k] = jnp.zeros((13, 16, 128), BF16)

    loads[2].wait()
    loads[3].wait()
    nil = jnp.zeros((64, 64), BF16)
    nil_half = jnp.zeros((256, 128), BF16)

    def band(layer):
        for yd in range(3):
            W[layer, yd * 256 : yd * 256 + 256, 128:256] = nil_half
            W[layer, (9 + yd) * 256 : (9 + yd) * 256 + 256, 0:128] = nil_half
        for zd in range(3):
            for yd in range(3):
                w0, w1, w2 = (wv[layer, 9 * zd + 3 * yd + k] for k in range(3))
                block = jnp.concatenate(
                    [
                        jnp.concatenate(ab, axis=1)
                        for ab in ((w1, w0), (w2, w1), (nil, w2), (w0, nil))
                    ],
                    axis=0,
                )
                at = (zd * 3 + yd) * 256
                W[layer, at : at + 256, 0:128] = block
                at = at + 768
                W[layer, at : at + 256, 128:256] = block

    band(0)

    here = lo.astype(jnp.int32) + hi.astype(jnp.int32) + be.astype(jnp.int32) + af.astype(jnp.int32)
    pl.semaphore_wait(barrier, here)

    def remote(src, dst, send, recv, to):
        return pltpu.make_async_remote_copy(
            src_ref=src, dst_ref=dst, send_sem=send, recv_sem=recv, device_id=to, device_id_type=MESH
        )

    upward = remote(msg.at[0], rmsg.at[0], msend.at[0], mrecv.at[0], {"space": s + 1})
    downward = remote(msg.at[1], rmsg.at[1], msend.at[1], mrecv.at[1], {"space": s - 1})

    @pl.when(hi)
    def _():
        upward.start()

    @pl.when(lo)
    def _():
        downward.start()

    band(1)

    def inner_rows(H, S, b):
        t = []
        for g in range(4):
            t.append(three(tile(H, b, g), rim_tile(H, b, 2, g), rim_tile(H, b, 3, g), row))
        for dy in range(3):
            put_layers(S, dy, b, INNER, slice(0, 128), pair(t[1][dy], t[2][dy]))
            e1 = jnp.where(left, t[2][dy], t[0][dy])
            e2 = jnp.where(left, t[3][dy], t[1][dy])
            put_layers(S, dy, b, INNER, slice(128, 256), pair(e1, e2))
        for face, at in ((4, (0, 0)), (5, (1, 4))):
            t = [three(rim_layer(H, b, face, g), 0.0, 0.0, row2) for g in range(4)]
            for dy in range(3):
                S[at[0], dy, b, at[1], INNER, 0:128] = pair(t[1][dy], t[2][dy])
                e1 = jnp.where(left[0], t[2][dy], t[0][dy])
                e2 = jnp.where(left[0], t[3][dy], t[1][dy])
                S[at[0], dy, b, at[1], INNER, 128:256] = pair(e1, e2)

    def outer_rows(H, S, b, xl, xr):
        t = {}
        for g in range(4):
            t[g] = three(tile(H, b, g), rim_tile(H, b, 2, g), rim_tile(H, b, 3, g), row)
        xl = three(xl, 0.0, 0.0, row)
        xr = three(xr, 0.0, 0.0, row)
        for dy in range(3):
            put_layers(S, dy, b, OUTER, slice(0, 128), pair(t[0][dy], t[3][dy]))
            e0 = jnp.where(left, t[1][dy], xl[dy])
            e3 = jnp.where(left, xr[dy], t[2][dy])
            put_layers(S, dy, b, OUTER, slice(128, 256), pair(e0, e3))
        for face, at in ((4, (0, 0)), (5, (1, 4))):
            t = [three(rim_layer(H, b, face, g), 0.0, 0.0, row2) for g in range(4)]
            for dy in range(3):
                S[at[0], dy, b, at[1], OUTER, 0:128] = pair(t[0][dy], t[3][dy])
                e0 = jnp.where(left[0], t[1][dy], 0.0)
                e3 = jnp.where(left[0], 0.0, t[2][dy])
                S[at[0], dy, b, at[1], OUTER, 128:256] = pair(e0, e3)

    @pl.loop(0, 4)
    def _(b):
        inner_rows(H0, S1, b)
        outer_rows(H0, S1, b, rim_tile(H0, b, 0, 3), rim_tile(H0, b, 1, 0))

    bias = [jnp.concatenate([bv[i : i + 1, :]] * 2, axis=1).reshape(1, 1, 1, 128) for i in range(2)]

    acc = jnp.dot(left_side(S1, slice(0, 32)), W[0], preferred_element_type=F32)
    acc = acc.reshape(4, 4, 4, 8, 256)
    for i, g in enumerate(PAIRS):
        for oz in range(2):
            h = acc[:, :, i, :, oz * 128 : (oz + 1) * 128] + bias[0]
            if i >= 2:
                ACC[:, :, oz, i - 2] = h
            H1[:, :, oz, g] = jnp.maximum(h, 0.0) * M[:, :, oz, g]

    @pl.loop(0, 4)
    def _(b):
        inner_rows(H1, S2, b)

    def second(half):
        rows = (INNER, OUTER)[half]
        acc = jnp.dot(left_side(S2, rows), W[1], preferred_element_type=F32)
        acc = acc.reshape(4, 4, 2, 8, 256)
        for i in range(2):
            g = PAIRS[2 * half + i]
            h = [
                jnp.maximum(acc[:, :, i, :, oz * 128 : (oz + 1) * 128] + bias[1], 0.0)
                * M[:, :, oz, g]
                for oz in range(2)
            ]
            H2[half, :, :, :, i * 128 : (i + 1) * 128] = jnp.concatenate(h, axis=2).astype(BF16)

    def exchange(half, sent, got, send, recv):
        for k in range(3):
            sent[0, k] = H2[half, sahead[0, k]]
            sent[1, k] = H2[half, sback[0, k]]
        ahead = remote(sent.at[0], got.at[0], send.at[0], recv.at[0], {"frame": f + 1})
        back = remote(sent.at[1], got.at[1], send.at[1], recv.at[1], {"frame": f - 1})

        @pl.when(af)
        def _():
            ahead.start()

        @pl.when(be)
        def _():
            back.start()

        return ahead, back

    second(0)
    early = exchange(0, sE, rE, esend, erecv)

    loads[4].wait()
    for k in range(3):
        w = wtv[k]
        two = jnp.concatenate(
            [jnp.concatenate([w, nil], axis=1), jnp.concatenate([nil, w], axis=1)], axis=0
        )
        WT[k, 0:128, 0:128] = two
        WT[k, 128:256, 128:256] = two
        WT[k, 0:128, 128:256] = jnp.zeros((128, 128), BF16)
        WT[k, 128:256, 0:128] = jnp.zeros((128, 128), BF16)

    def wide(H, g):
        return H[:, :, :, g].reshape(4, 4, 16, 128)

    def base(half):
        t = jnp.dot(H2[half].reshape(256, 256), WT[1], preferred_element_type=F32)
        t = t.reshape(4, 4, 16, 256)
        for i in range(2):
            g = PAIRS[2 * half + i]
            lanes = slice(i * 128, (i + 1) * 128)
            BASE[half, :, :, :, lanes] = t[:, :, :, lanes] + wide(H0, g)

    base(0)

    for there, copy in ((lo, upward), (hi, downward)):

        @pl.when(there)
        def _(copy=copy):
            copy.wait_recv()

    def parts(k):
        x = rmsg[k].astype(F32)
        return (
            x[0:4].reshape(8, 8, 128),
            x[4:8].reshape(8, 8, 128),
            x[8:12].reshape(8, 8, 128),
            x[12].reshape(2, 8, 128),
        )

    got = [parts(0), parts(1)]
    own = (tile(H0, down, 0), tile(H0, up, 3))
    V = []
    for k in range(2):
        a, b, e, z = got[k]
        beyond = jnp.where(e[:, 3:4, :] > 0.5, own[k], b)
        V.append((three(a, e, e, row), three(beyond, 0.0, 0.0, row), three(z, 0.0, 0.0, row)))
    zero = jnp.zeros((8, 8, 128), F32)
    thin = jnp.zeros((16, 128), BF16)
    for dy in range(3):
        put_layers(SV, dy, 0, INNER, slice(0, 128), pair(V[0][0][dy], V[1][0][dy]))
        put_layers(SV, dy, 0, INNER, slice(128, 256), pair(V[0][1][dy], V[1][1][dy]))
        put_layers(SV, dy, 0, OUTER, slice(0, 128), pair(zero, zero))
        x0 = jnp.where(left, 0.0, three(got[0][0], 0.0, 0.0, row)[dy])
        x1 = jnp.where(left, three(got[1][0], 0.0, 0.0, row)[dy], 0.0)
        put_layers(SV, dy, 0, OUTER, slice(128, 256), pair(x0, x1))
        for z, at in ((0, (0, 0)), (1, (1, 4))):
            SV[at[0], dy, 0, at[1], INNER, 0:128] = pair(V[0][2][dy][z], V[1][2][dy][z])
            SV[at[0], dy, 0, at[1], INNER, 128:256] = thin
            SV[at[0], dy, 0, at[1], OUTER, 0:128] = thin
            SV[at[0], dy, 0, at[1], OUTER, 128:256] = thin

    acc = jnp.dot(left_side(SV, slice(0, 32)), W[0], preferred_element_type=F32)
    acc = acc.reshape(4, 4, 8, 256)
    for k in range(2):
        for oz in range(2):
            lanes = slice(oz * 128, (oz + 1) * 128)
            mask = got[k][1].reshape(4, 2, 8, 128)[:, oz]
            VH[k, :, oz] = jnp.maximum(acc[:, k, :, lanes] + bias[0][0], 0.0) * mask
            CR[k, :, oz] = acc[:, 2 + k, :, lanes]

    @pl.loop(0, 4)
    def _(b):
        for k, g in ((0, 0), (1, 3)):
            h = ACC[b, :, :, k] + jnp.where(fsrc[0, b, k] == k, CR[k], 0.0)
            H1[b, :, :, g] = jnp.maximum(h, 0.0) * M[b, :, :, g]

    @pl.loop(0, 4)
    def _(b):
        x = []
        for k, g in ((0, 3), (1, 0)):
            far = VH[k].reshape(8, 8, 128)
            x.append(jnp.where(fsrc[0, b, k] == k, far, rim_tile(H1, b, k, g)))
        outer_rows(H1, S2, b, x[0], x[1])

    second(1)
    late = exchange(1, sL, rL, lsend, lrecv)
    base(1)

    def finish(half, copies, got):
        ahead, back = copies

        @pl.when(be)
        def _():
            ahead.wait_recv()

        @pl.when(af)
        def _():
            back.wait_recv()

        lhs = []
        for b in range(4):
            p, q = fprior[0, b], flater[0, b]
            x = jnp.where(p >= 0, got[0, jnp.maximum(p, 0)].astype(F32), 0.0).astype(BF16)
            y = jnp.where(q >= 0, got[1, jnp.maximum(q, 0)].astype(F32), 0.0).astype(BF16)
            lhs.append(jnp.concatenate([x.reshape(64, 256), y.reshape(64, 256)], axis=1))
        wt = jnp.concatenate([WT[0], WT[2]], axis=0)
        t = jnp.dot(jnp.concatenate(lhs, axis=0), wt, preferred_element_type=F32)
        t = t.reshape(4, 4, 16, 256)
        for i in range(2):
            g = PAIRS[2 * half + i]
            lanes = slice(i * 128, (i + 1) * 128)
            x = (BASE[half, :, :, :, lanes] + t[:, :, :, lanes]) * wide(M, g)
            out[0, :, :, :, g * 128 : (g + 1) * 128] = x.reshape(4, 8, 8, 128).astype(BF16)

    finish(0, early, rE)
    finish(1, late, rL)

    for there, copies in (
        (hi, (upward,)),
        (lo, (downward,)),
        (af, (early[0], late[0])),
        (be, (early[1], late[1])),
    ):

        @pl.when(there)
        def _(copies=copies):
            for c in copies:
                c.wait_send()


def per_device(*args):
    field = (4, 4, 2, 4, 8, 128)
    hbm = pl.BlockSpec(memory_space=pltpu.HBM)
    smem = pl.BlockSpec(memory_space=pltpu.SMEM)
    left = (2, 3, 4, 5, 32, 256)
    parcels = (2, 3, 4, 16, 256)
    return pl.pallas_call(
        kernel,
        out_shape=pltpu.VMEM((1, 4, 8, 8, 512), BF16),
        in_specs=[hbm] * 5 + [smem] * 6,
        out_specs=pl.BlockSpec(memory_space=pltpu.VMEM),
        scratch_shapes=[
            pltpu.VMEM((4, 8, 8, 512), BF16),
            pltpu.VMEM((4, 512), jnp.int32),
            pltpu.VMEM((2, 27, 64, 64), BF16),
            pltpu.VMEM((2, 64), F32),
            pltpu.VMEM((3, 64, 64), BF16),
            pltpu.VMEM(field, F32),
            pltpu.VMEM(field, F32),
            pltpu.VMEM(field, F32),
            pltpu.VMEM((4, 4, 2, 2, 8, 128), F32),
            pltpu.VMEM(left, BF16),
            pltpu.VMEM(left, BF16),
            pltpu.VMEM((2, 3, 1, 5, 32, 256), BF16),
            pltpu.VMEM((2, 3072, 256), BF16),
            pltpu.VMEM((3, 256, 256), BF16),
            pltpu.VMEM((2, 4, 2, 8, 128), F32),
            pltpu.VMEM((2, 4, 2, 8, 128), F32),
            pltpu.VMEM((2, 13, 16, 128), BF16),
            pltpu.VMEM((2, 13, 16, 128), BF16),
            pltpu.VMEM(parcels, BF16),
            pltpu.VMEM(parcels, BF16),
            pltpu.VMEM(parcels, BF16),
            pltpu.VMEM(parcels, BF16),
            pltpu.VMEM((2, 4, 4, 16, 256), BF16),
            pltpu.VMEM((2, 4, 4, 16, 256), F32),
            pltpu.SemaphoreType.DMA((5,)),
        ]
        + [pltpu.SemaphoreType.DMA((2,))] * 6,
        compiler_params=pltpu.CompilerParams(
            collective_id=0, has_side_effects=True, vmem_limit_bytes=40 << 20
        ),
    )(*args)


def solution(mesh):
    in_specs = (
        P("frame", "space", None, None, None),
        P("frame", "space", None),
        P(),
        P(),
        P(),
        P("frame", "space"),
        P("frame", "space", None),
        P("frame", "space"),
        P("frame", "space"),
        P("frame", "space"),
        P("frame", "space"),
    )
    out_specs = P("frame", "space", None, None, None)
    return jax.shard_map(
        per_device, mesh=mesh, in_specs=in_specs, out_specs=out_specs, check_vma=False
    )
```

time: 303 us -> 24.5 us (0.08)
  local copies, waits for them, and re-layouts: 243 us -> 8.95 us
  starting transfers between devices: 20.9 us -> 0 us
  matrix products: 20.3 us -> 0 us
  Pallas kernels: 0 us -> 15.2 us
  other arithmetic: 11 us -> 0 us
  waiting for transfers between devices: 3.57 us -> 0 us
    while x132 -> x0, local copies, waits for them, and re-layouts: 83.6 us -> none
    another operation x145 -> x0, local copies, waits for them, and re-layouts: 67.7 us -> none  [the longest x112 61.4 us: one_group(): jnp.stack(shifted, axis=1)]
    scatter x14 -> x0, local copies, waits for them, and re-layouts: 67.1 us -> none  [the longest x2 20.2 us: padded_block(): padded.at[:, inner, inner, (edge_len + 1) * channels:wide_cols]]
    ppermute x6 -> x0, starting transfers between devices: 20.9 us -> none  [passed_along(): return lax.ppermute(x, axis, pairs)]
    dot_general x7 -> x0, matrix products: 20.3 us -> none  [the longest x4 19.3 us: one_group(): jnp.einsum('btzyxc,tcd->bzyxd', columns, weights, preferred_element_type=...]
    pallas_call x0 -> x1, Pallas kernels: none -> 15.2 us  [per_device(): pl.pallas_call(kernel, out_shape=pltpu.VMEM((1, 4, 8, 8, 512), BF16), in_...]
    slice x21 -> x0, local copies, waits for them, and re-layouts: 9.6 us -> none  [the longest x8 8.27 us: one_group(): piece_block[:, depth_off:depth_off + edge_len, row_off:row_off + edge_len...]
    unnamed x32 -> x23, local copies, waits for them, and re-layouts: 0.12 us -> 8.95 us
  transfers between devices with their start and end apart: 6 -> 0, of which waited for: 2 -> 0; matrix products, arithmetic and copies ran while one was open for 5% -> 0% of each run, Pallas kernels for 0% -> 0%
where the time goes in v1:
time: 24.5 us; the launch traced here: 24.2 us
  Pallas kernels  15.2 us (62%)
  local copies, waits for them, and re-layouts  8.95 us (37%)
    pallas_call x1, Pallas kernels, per_device(): pl.pallas_call(kernel, out_shape=pltpu.VMEM((1, 4, 8, 8, 512), BF16), in_...  15.2 us
    unnamed x23, local copies, waits for them, and re-layouts  8.95 us

profile of v1, /device:TPU:120, one launch (start us, length us, event | category | flops | bytes accessed | tf_op | source)
XLA Modules:
  0.0 24.2 jit_solution(4994800753568962588)
XLA Ops:
  0.0 0.0 copy-start
  0.0 1.2 %copy-done = bf16[2,27,64,64]{3,2,1,0:T(8,128)(2,1)S(1)} copy-done((bf16[2,27,64,64]{3,2,1,0:T(8,128)(2,1)S(1)}, bf16[2,27,64,64]{3,2,1,0:T(8,128)(2,1)}, u32[]{:S(2)}) %copy-start) | copy-done | bytes 442392
  1.2 0.0 copy-start.1
  1.2 0.9 %copy-done.1 = bf16[1,4,8,8,512]{4,3,2,1,0:T(8,128)(2,1)S(1)} copy-done((bf16[1,4,8,8,512]{4,3,2,1,0:T(8,128)(2,1)S(1)}, bf16[1,4,8,8,512]{4,3,2,1,0:T(8,128)(2,1)}, u32[]{:S(2)}) %copy-start.1) | copy-done | bytes 262168
  2.1 0.0 copy-start.2
  2.1 0.8 %copy-done.2 = bf16[3,64,64]{2,1,0:T(8,128)(2,1)S(1)} copy-done((bf16[3,64,64]{2,1,0:T(8,128)(2,1)S(1)}, bf16[3,64,64]{2,1,0:T(8,128)(2,1)}, u32[]{:S(2)}) %copy-start.2) | copy-done | bytes 24600
  2.9 0.0 copy-start.3
  2.9 0.7 %copy-done.3 = s32[1,4,512]{2,1,0:T(4,128)S(1)} copy-done((s32[1,4,512]{2,1,0:T(4,128)S(1)}, s32[1,4,512]{2,1,0:T(4,128)}, u32[]{:S(2)}) %copy-start.3) | copy-done | bytes 8216
  3.6 0.0 copy-start.4
  3.6 0.7 %copy-done.4 = s32[1,4,6]{2,1,0:T(4,128)S(1)} copy-done((s32[1,4,6]{2,1,0:T(4,128)S(1)}, s32[1,4,6]{2,1,0:T(4,128)}, u32[]{:S(2)}) %copy-start.4) | copy-done | bytes 120
  4.3 0.0 copy-start.5
  4.3 0.7 %copy-done.5 = f32[2,64]{1,0:T(2,128)S(1)} copy-done((f32[2,64]{1,0:T(2,128)S(1)}, f32[2,64]{1,0:T(2,128)}, u32[]{:S(2)}) %copy-start.5) | copy-done | bytes 536
  5.0 0.0 copy-start.6
  5.0 0.7 %copy-done.6 = s32[1,2]{1,0:T(1,128)S(1)} copy-done((s32[1,2]{1,0:T(1,128)S(1)}, s32[1,2]{1,0:T(1,128)}, u32[]{:S(2)}) %copy-start.6) | copy-done | bytes 32
  5.6 0.0 copy-start.7
  5.6 0.7 %copy-done.7 = s32[1,3]{1,0:T(1,128)S(1)} copy-done((s32[1,3]{1,0:T(1,128)S(1)}, s32[1,3]{1,0:T(1,128)}, u32[]{:S(2)}) %copy-start.7) | copy-done | bytes 36
  6.3 0.0 copy-start.8
  6.3 0.7 %copy-done.8 = s32[1,4]{1,0:T(1,128)S(1)} copy-done((s32[1,4]{1,0:T(1,128)S(1)}, s32[1,4]{1,0:T(1,128)}, u32[]{:S(2)}) %copy-start.8) | copy-done | bytes 40
  6.9 0.0 copy-start.9
  6.9 0.7 %copy-done.9 = s32[1,3]{1,0:T(1,128)S(1)} copy-done((s32[1,3]{1,0:T(1,128)S(1)}, s32[1,3]{1,0:T(1,128)}, u32[]{:S(2)}) %copy-start.9) | copy-done | bytes 36
  7.6 0.0 copy-start.10
  7.6 0.7 %copy-done.10 = s32[1,4]{1,0:T(1,128)S(1)} copy-done((s32[1,4]{1,0:T(1,128)S(1)}, s32[1,4]{1,0:T(1,128)}, u32[]{:S(2)}) %copy-start.10) | copy-done | bytes 40
  8.3 15.2 %shard_map.109 = bf16[1,4,8,8,512]{4,3,2,1,0:T(8,128)(2,1)S(1)} custom-call(bf16[1,4,8,8,512]{4,3,2,1,0:T(8,128)(2,1)S(1)} %copy-done.1, s32[1,4,512]{2,1,0:T(4,128)S(1)} %copy-done.3, bf16[2,27,64,64]{3,2,1,0:T(8,128)(2,1)S(1)} %copy-done, f32[2,64]{1,0:T(2,128)S(1)} %copy-done.5, bf16[3,64,64]{2,1,0:T(8,128)(2,1)S(1)} %copy-done.2, s32[1,2]{1,0:T(1,128)S(1)} %copy-done.6, ...), custom_call_target="tpu_custom_call" | custom-call | tf_op jit(solution)/shard_map/pallas_call | solution.py:415
  23.5 0.7 %copy.13 = bf16[1,4,8,8,512]{4,3,2,1,0:T(8,128)(2,1)} copy(bf16[1,4,8,8,512]{4,3,2,1,0:T(8,128)(2,1)S(1)} %shard_map.109) | data formatting | bytes 524288
Async XLA Ops:
  0.0 1.2 %copy-start = (bf16[2,27,64,64]{3,2,1,0:T(8,128)(2,1)S(1)}, bf16[2,27,64,64]{3,2,1,0:T(8,128)(2,1)}, u32[]{:S(2)}) copy-start(bf16[2,27,64,64]{3,2,1,0:T(8,128)(2,1)} %wsp.1) | copy-start | bytes 1327108
  1.2 0.9 %copy-start.1 = (bf16[1,4,8,8,512]{4,3,2,1,0:T(8,128)(2,1)S(1)}, bf16[1,4,8,8,512]{4,3,2,1,0:T(8,128)(2,1)}, u32[]{:S(2)}) copy-start(bf16[1,4,8,8,512]{4,3,2,1,0:T(8,128)(2,1)} %feats.1) | copy-start | bytes 786436
  2.1 0.8 %copy-start.2 = (bf16[3,64,64]{2,1,0:T(8,128)(2,1)S(1)}, bf16[3,64,64]{2,1,0:T(8,128)(2,1)}, u32[]{:S(2)}) copy-start(bf16[3,64,64]{2,1,0:T(8,128)(2,1)} %wtm.1) | copy-start | bytes 73732
  2.9 0.7 %copy-start.3 = (s32[1,4,512]{2,1,0:T(4,128)S(1)}, s32[1,4,512]{2,1,0:T(4,128)}, u32[]{:S(2)}) copy-start(s32[1,4,512]{2,1,0:T(4,128)} %occ.1) | copy-start | bytes 24580
  3.6 0.7 %copy-start.4 = (s32[1,4,6]{2,1,0:T(4,128)S(1)}, s32[1,4,6]{2,1,0:T(4,128)}, u32[]{:S(2)}) copy-start(s32[1,4,6]{2,1,0:T(4,128)} %fsrc.1) | copy-start | bytes 292
  4.3 0.7 %copy-start.5 = (f32[2,64]{1,0:T(2,128)S(1)}, f32[2,64]{1,0:T(2,128)}, u32[]{:S(2)}) copy-start(f32[2,64]{1,0:T(2,128)} %bsp.1) | copy-start | bytes 1540
  5.0 0.7 %copy-start.6 = (s32[1,2]{1,0:T(1,128)S(1)}, s32[1,2]{1,0:T(1,128)}, u32[]{:S(2)}) copy-start(s32[1,2]{1,0:T(1,128)} %fsend.1) | copy-start | bytes 28
  5.6 0.7 %copy-start.7 = (s32[1,3]{1,0:T(1,128)S(1)}, s32[1,3]{1,0:T(1,128)}, u32[]{:S(2)}) copy-start(s32[1,3]{1,0:T(1,128)} %sahead.1) | copy-start | bytes 40
  6.3 0.7 %copy-start.8 = (s32[1,4]{1,0:T(1,128)S(1)}, s32[1,4]{1,0:T(1,128)}, u32[]{:S(2)}) copy-start(s32[1,4]{1,0:T(1,128)} %fprior.1) | copy-start | bytes 52
  6.9 0.7 %copy-start.9 = (s32[1,3]{1,0:T(1,128)S(1)}, s32[1,3]{1,0:T(1,128)}, u32[]{:S(2)}) copy-start(s32[1,3]{1,0:T(1,128)} %sback.1) | copy-start | bytes 40
  7.6 0.7 %copy-start.10 = (s32[1,4]{1,0:T(1,128)S(1)}, s32[1,4]{1,0:T(1,128)}, u32[]{:S(2)}) copy-start(s32[1,4]{1,0:T(1,128)} %flater.1) | copy-start | bytes 52

commit v2 on v1

--- a/solution.py
+++ b/solution.py
@@ -44,8 +44,8 @@
 
 
 def kernel(
-    feats, occ, wsp, bsp, wtm, fsend, fsrc, sahead, fprior, sback, flater, out,
-    fin, occv, wv, bv, wtv, M, H0, H1, ACC, S1, S2, SV, W, WT, VH, CR, msg, rmsg,
+    feats, occ, wsp, bsp, wtm, fsend_h, fsrc_h, sahead_h, fprior_h, sback_h, flater_h, out,
+    fsend, fsrc, sahead, fprior, sback, flater, fin, occv, wv, bv, wtv, M, H0, H1, ACC, S1, S2, SV, W, WT, VH, CR, msg, rmsg,
     sE, rE, sL, rL, H2, BASE, lsem, msend, mrecv, esend, erecv, lsend, lrecv,
 ):
     s, f = lax.axis_index("space"), lax.axis_index("frame")
@@ -55,7 +55,11 @@
     loads = [
         pltpu.make_async_copy(src, dst, lsem.at[i])
         for i, (src, dst) in enumerate(
-            ((occ.at[0], occv), (feats.at[0], fin), (wsp, wv), (bsp, bv), (wtm, wtv))
+            (
+                (occ.at[0], occv), (feats.at[0], fin), (wsp, wv), (bsp, bv), (wtm, wtv),
+                (fsend_h, fsend), (fsrc_h, fsrc), (sahead_h, sahead), (fprior_h, fprior),
+                (sback_h, sback), (flater_h, flater),
+            )
         )
     ]
     for c in loads:
@@ -96,6 +100,9 @@
         M[:, :, :, g] = mg
         x = fin[:, :, :, g * 128 : (g + 1) * 128].astype(F32)
         H0[:, :, :, g] = x.reshape(4, 4, 2, 8, 128) * mg
+
+    for copy in loads[5:]:
+        copy.wait()
 
     def tile(H, b, g):
         return H[b, :, :, g].reshape(8, 8, 128)
@@ -409,15 +416,20 @@
 def per_device(*args):
     field = (4, 4, 2, 4, 8, 128)
     hbm = pl.BlockSpec(memory_space=pltpu.HBM)
-    smem = pl.BlockSpec(memory_space=pltpu.SMEM)
     left = (2, 3, 4, 5, 32, 256)
     parcels = (2, 3, 4, 16, 256)
     return pl.pallas_call(
         kernel,
         out_shape=pltpu.VMEM((1, 4, 8, 8, 512), BF16),
-        in_specs=[hbm] * 5 + [smem] * 6,
+        in_specs=[hbm] * 11,
         out_specs=pl.BlockSpec(memory_space=pltpu.VMEM),
         scratch_shapes=[
+            pltpu.SMEM((1, 2), jnp.int32),
+            pltpu.SMEM((1, 4, 6), jnp.int32),
+            pltpu.SMEM((1, 3), jnp.int32),
+            pltpu.SMEM((1, 4), jnp.int32),
+            pltpu.SMEM((1, 3), jnp.int32),
+            pltpu.SMEM((1, 4), jnp.int32),
             pltpu.VMEM((4, 8, 8, 512), BF16),
             pltpu.VMEM((4, 512), jnp.int32),
             pltpu.VMEM((2, 27, 64, 64), BF16),
@@ -442,11 +454,11 @@
             pltpu.VMEM(parcels, BF16),
             pltpu.VMEM((2, 4, 4, 16, 256), BF16),
             pltpu.VMEM((2, 4, 4, 16, 256), F32),
-            pltpu.SemaphoreType.DMA((5,)),
+            pltpu.SemaphoreType.DMA((11,)),
         ]
         + [pltpu.SemaphoreType.DMA((2,))] * 6,
         compiler_params=pltpu.CompilerParams(
-            collective_id=0, has_side_effects=True, vmem_limit_bytes=40 << 20
+            collective_id=0, has_side_effects=True, vmem_limit_bytes=56 << 20
         ),
     )(*args)
 

time: 24.5 us -> 15.2 us (0.62)
  local copies, waits for them, and re-layouts: 8.95 us -> 0.71 us
  Pallas kernels: 15.2 us -> 14.4 us
    unnamed x23 -> x1, local copies, waits for them, and re-layouts: 8.95 us -> 0.71 us
    pallas_call x1, Pallas kernels: 15.2 us -> 14.4 us  [per_device(): pl.pallas_call(kernel, out_shape=pltpu.VMEM((1, 4, 8, 8, 512), BF16), in_...]
where the time goes in v2:
time: 15.2 us; the launch traced here: 15.1 us
  Pallas kernels  14.4 us (95%)
  local copies, waits for them, and re-layouts  0.71 us (5%)
    pallas_call x1, Pallas kernels, per_device(): pl.pallas_call(kernel, out_shape=pltpu.VMEM((1, 4, 8, 8, 512), BF16), in_...  14.4 us
    unnamed x1, local copies, waits for them, and re-layouts  0.71 us

profile of v2, /device:TPU:120, one launch (start us, length us, event | category | flops | bytes accessed | tf_op | source)
XLA Modules:
  0.0 15.1 jit_solution(7672798819754911518)
XLA Ops:
  0.0 14.4 %shard_map.109 = bf16[1,4,8,8,512]{4,3,2,1,0:T(8,128)(2,1)S(1)} custom-call(bf16[1,4,8,8,512]{4,3,2,1,0:T(8,128)(2,1)} %feats.1, s32[1,4,512]{2,1,0:T(4,128)} %occ.1, bf16[2,27,64,64]{3,2,1,0:T(8,128)(2,1)} %wsp.1, f32[2,64]{1,0:T(2,128)} %bsp.1, bf16[3,64,64]{2,1,0:T(8,128)(2,1)} %wtm.1, s32[1,2]{1,0:T(1,128)} %fsend_h.1, s32[1,4,6]{2,1,0:T(4,128)} %fsrc_h.1, ...), custom_call_target="tpu_custom_call" | custom-call | tf_op jit(solution)/shard_map/pallas_call | solution.py:421
  14.4 0.7 %copy.13 = bf16[1,4,8,8,512]{4,3,2,1,0:T(8,128)(2,1)} copy(bf16[1,4,8,8,512]{4,3,2,1,0:T(8,128)(2,1)S(1)} %shard_map.109) | data formatting | bytes 524288

commit v3 on v2

--- a/solution.py
+++ b/solution.py
@@ -34,19 +34,20 @@
     S[0, dy, at, 1:5, rows, lanes] = x[:, 1]
 
 
-def left_side(S, rows):
+def left_side(S, rows, start=0, count=4):
     pieces = []
     for zz in range(4):
         for dy in range(3):
-            x = S[zz % 2, dy, :, zz // 2 : zz // 2 + 4, rows, :]
+            at = zz // 2 + start
+            x = S[zz % 2, dy, :, at : at + count, rows, :]
             pieces.append(x.reshape(-1, 256))
     return jnp.concatenate(pieces, axis=1)
 
 
 def kernel(
     feats, occ, wsp, bsp, wtm, fsend_h, fsrc_h, sahead_h, fprior_h, sback_h, flater_h, out,
-    fsend, fsrc, sahead, fprior, sback, flater, fin, occv, wv, bv, wtv, M, H0, H1, ACC, S1, S2, SV, W, WT, VH, CR, msg, rmsg,
-    sE, rE, sL, rL, H2, BASE, lsem, msend, mrecv, esend, erecv, lsend, lrecv,
+    fsend, fsrc, sahead, fprior, sback, flater, fin, occv, wv, bv, wtv, M, H0, H1, ACC, S1, S2, SV, W0, W1, WT, VH, CR, msg, rmsg,
+    sE, rE, sL, rL0, rL1, H2, BASE, lsem, msend, mrecv, esend, erecv, lsend, lrecv,
 ):
     s, f = lax.axis_index("space"), lax.axis_index("frame")
     n_s, n_f = lax.axis_size("space"), lax.axis_size("frame")
@@ -152,10 +153,12 @@
     nil = jnp.zeros((64, 64), BF16)
     nil_half = jnp.zeros((256, 128), BF16)
 
+    W = (W0, W1)
+
     def band(layer):
         for yd in range(3):
-            W[layer, yd * 256 : yd * 256 + 256, 128:256] = nil_half
-            W[layer, (9 + yd) * 256 : (9 + yd) * 256 + 256, 0:128] = nil_half
+            W[layer][yd * 256 : yd * 256 + 256, 128:256] = nil_half
+            W[layer][(9 + yd) * 256 : (9 + yd) * 256 + 256, 0:128] = nil_half
         for zd in range(3):
             for yd in range(3):
                 w0, w1, w2 = (wv[layer, 9 * zd + 3 * yd + k] for k in range(3))
@@ -167,9 +170,9 @@
                     axis=0,
                 )
                 at = (zd * 3 + yd) * 256
-                W[layer, at : at + 256, 0:128] = block
+                W[layer][at : at + 256, 0:128] = block
                 at = at + 768
-                W[layer, at : at + 256, 128:256] = block
+                W[layer][at : at + 256, 128:256] = block
 
     band(0)
 
@@ -191,8 +194,6 @@
     @pl.when(lo)
     def _():
         downward.start()
-
-    band(1)
 
     def inner_rows(H, S, b):
         t = []
@@ -211,33 +212,38 @@
                 e2 = jnp.where(left[0], t[3][dy], t[1][dy])
                 S[at[0], dy, b, at[1], INNER, 128:256] = pair(e1, e2)
 
+    row16 = lax.broadcasted_iota(jnp.int32, (16, 128), 0)
+    lane16 = lax.broadcasted_iota(jnp.int32, (16, 128), 1)
+    near = (row16 < 8) == (lane16 < 64)
+
     def outer_rows(H, S, b, xl, xr):
-        t = {}
-        for g in range(4):
-            t[g] = three(tile(H, b, g), rim_tile(H, b, 2, g), rim_tile(H, b, 3, g), row)
+        t = [
+            three(tile(H, b, g), rim_tile(H, b, 2, g), rim_tile(H, b, 3, g), row) for g in (0, 3)
+        ]
         xl = three(xl, 0.0, 0.0, row)
         xr = three(xr, 0.0, 0.0, row)
         for dy in range(3):
-            put_layers(S, dy, b, OUTER, slice(0, 128), pair(t[0][dy], t[3][dy]))
-            e0 = jnp.where(left, t[1][dy], xl[dy])
-            e3 = jnp.where(left, xr[dy], t[2][dy])
-            put_layers(S, dy, b, OUTER, slice(128, 256), pair(e0, e3))
+            put_layers(S, dy, b, OUTER, slice(0, 128), pair(t[0][dy], t[1][dy]))
+            far = pair(xl[dy], xr[dy]).reshape(4, 2, 16, 128)
+            for odd, at in ((0, slice(0, 4)), (1, slice(1, 5))):
+                inner = S[1 - odd, dy, b, at, INNER, 0:128]
+                S[1 - odd, dy, b, at, OUTER, 128:256] = jnp.where(near, inner, far[:, odd])
         for face, at in ((4, (0, 0)), (5, (1, 4))):
-            t = [three(rim_layer(H, b, face, g), 0.0, 0.0, row2) for g in range(4)]
+            t = [three(rim_layer(H, b, face, g), 0.0, 0.0, row2) for g in (0, 3)]
             for dy in range(3):
-                S[at[0], dy, b, at[1], OUTER, 0:128] = pair(t[0][dy], t[3][dy])
-                e0 = jnp.where(left[0], t[1][dy], 0.0)
-                e3 = jnp.where(left[0], 0.0, t[2][dy])
-                S[at[0], dy, b, at[1], OUTER, 128:256] = pair(e0, e3)
-
-    @pl.loop(0, 4)
+                S[at[0], dy, b, at[1], OUTER, 0:128] = pair(t[0][dy], t[1][dy])
+                inner = S[at[0], dy, b, at[1], INNER, 0:128]
+                S[at[0], dy, b, at[1], OUTER, 128:256] = jnp.where(near, inner, jnp.zeros((), BF16))
+
+    @pl.loop(0, 4, unroll=True)
     def _(b):
         inner_rows(H0, S1, b)
         outer_rows(H0, S1, b, rim_tile(H0, b, 0, 3), rim_tile(H0, b, 1, 0))
 
     bias = [jnp.concatenate([bv[i : i + 1, :]] * 2, axis=1).reshape(1, 1, 1, 128) for i in range(2)]
 
-    acc = jnp.dot(left_side(S1, slice(0, 32)), W[0], preferred_element_type=F32)
+    band(1)
+    acc = jnp.dot(left_side(S1, slice(0, 32)), W0[...], preferred_element_type=F32)
     acc = acc.reshape(4, 4, 4, 8, 256)
     for i, g in enumerate(PAIRS):
         for oz in range(2):
@@ -246,27 +252,29 @@
                 ACC[:, :, oz, i - 2] = h
             H1[:, :, oz, g] = jnp.maximum(h, 0.0) * M[:, :, oz, g]
 
-    @pl.loop(0, 4)
+    @pl.loop(0, 4, unroll=True)
     def _(b):
         inner_rows(H1, S2, b)
 
-    def second(half):
-        rows = (INNER, OUTER)[half]
-        acc = jnp.dot(left_side(S2, rows), W[1], preferred_element_type=F32)
-        acc = acc.reshape(4, 4, 2, 8, 256)
+    def second(half, start, count):
+        rows, layers = (INNER, OUTER)[half], slice(start, start + count)
+        acc = jnp.dot(left_side(S2, rows, start, count), W1[...], preferred_element_type=F32)
+        acc = acc.reshape(4, count, 2, 8, 256)
         for i in range(2):
             g = PAIRS[2 * half + i]
             h = [
                 jnp.maximum(acc[:, :, i, :, oz * 128 : (oz + 1) * 128] + bias[1], 0.0)
-                * M[:, :, oz, g]
+                * M[:, layers, oz, g]
                 for oz in range(2)
             ]
-            H2[half, :, :, :, i * 128 : (i + 1) * 128] = jnp.concatenate(h, axis=2).astype(BF16)
-
-    def exchange(half, sent, got, send, recv):
+            H2[half, :, layers, :, i * 128 : (i + 1) * 128] = jnp.concatenate(h, axis=2).astype(BF16)
+
+    def exchange(half, start, count, sent, got, sems):
+        layers = slice(start, start + count)
         for k in range(3):
-            sent[0, k] = H2[half, sahead[0, k]]
-            sent[1, k] = H2[half, sback[0, k]]
+            sent[0, k] = H2[half, sahead[0, k], layers]
+            sent[1, k] = H2[half, sback[0, k], layers]
+        send, recv = sems
         ahead = remote(sent.at[0], got.at[0], send.at[0], recv.at[0], {"frame": f + 1})
         back = remote(sent.at[1], got.at[1], send.at[1], recv.at[1], {"frame": f - 1})
 
@@ -280,32 +288,8 @@
 
         return ahead, back
 
-    second(0)
-    early = exchange(0, sE, rE, esend, erecv)
-
-    loads[4].wait()
-    for k in range(3):
-        w = wtv[k]
-        two = jnp.concatenate(
-            [jnp.concatenate([w, nil], axis=1), jnp.concatenate([nil, w], axis=1)], axis=0
-        )
-        WT[k, 0:128, 0:128] = two
-        WT[k, 128:256, 128:256] = two
-        WT[k, 0:128, 128:256] = jnp.zeros((128, 128), BF16)
-        WT[k, 128:256, 0:128] = jnp.zeros((128, 128), BF16)
-
-    def wide(H, g):
-        return H[:, :, :, g].reshape(4, 4, 16, 128)
-
-    def base(half):
-        t = jnp.dot(H2[half].reshape(256, 256), WT[1], preferred_element_type=F32)
-        t = t.reshape(4, 4, 16, 256)
-        for i in range(2):
-            g = PAIRS[2 * half + i]
-            lanes = slice(i * 128, (i + 1) * 128)
-            BASE[half, :, :, :, lanes] = t[:, :, :, lanes] + wide(H0, g)
-
-    base(0)
+    second(0, 0, 4)
+    early = exchange(0, 0, 4, sE, rE, (esend, erecv))
 
     for there, copy in ((lo, upward), (hi, downward)):
 
@@ -344,7 +328,7 @@
             SV[at[0], dy, 0, at[1], OUTER, 0:128] = thin
             SV[at[0], dy, 0, at[1], OUTER, 128:256] = thin
 
-    acc = jnp.dot(left_side(SV, slice(0, 32)), W[0], preferred_element_type=F32)
+    acc = jnp.dot(left_side(SV, slice(0, 32)), W0[...], preferred_element_type=F32)
     acc = acc.reshape(4, 4, 8, 256)
     for k in range(2):
         for oz in range(2):
@@ -353,13 +337,13 @@
             VH[k, :, oz] = jnp.maximum(acc[:, k, :, lanes] + bias[0][0], 0.0) * mask
             CR[k, :, oz] = acc[:, 2 + k, :, lanes]
 
-    @pl.loop(0, 4)
+    @pl.loop(0, 4, unroll=True)
     def _(b):
         for k, g in ((0, 0), (1, 3)):
             h = ACC[b, :, :, k] + jnp.where(fsrc[0, b, k] == k, CR[k], 0.0)
             H1[b, :, :, g] = jnp.maximum(h, 0.0) * M[b, :, :, g]
 
-    @pl.loop(0, 4)
+    @pl.loop(0, 4, unroll=True)
     def _(b):
         x = []
         for k, g in ((0, 3), (1, 0)):
@@ -367,12 +351,40 @@
             x.append(jnp.where(fsrc[0, b, k] == k, far, rim_tile(H1, b, k, g)))
         outer_rows(H1, S2, b, x[0], x[1])
 
-    second(1)
-    late = exchange(1, sL, rL, lsend, lrecv)
+    late = []
+    rL = (rL0, rL1)
+    for n in range(2):
+        second(1, 2 * n, 2)
+        late.append(exchange(1, 2 * n, 2, sL.at[n], rL[n], (lsend.at[n], lrecv.at[n])))
+    loads[4].wait()
+    for k in range(3):
+        w = wtv[k]
+        two = jnp.concatenate(
+            [jnp.concatenate([w, nil], axis=1), jnp.concatenate([nil, w], axis=1)], axis=0
+        )
+        WT[k, 0:128, 0:128] = two
+        WT[k, 128:256, 128:256] = two
+        WT[k, 0:128, 128:256] = jnp.zeros((128, 128), BF16)
+        WT[k, 128:256, 0:128] = jnp.zeros((128, 128), BF16)
+
+    def wide(H, g):
+        return H[:, :, :, g].reshape(4, 4, 16, 128)
+
+    def base(half):
+        t = jnp.dot(H2[half].reshape(256, 256), WT[1], preferred_element_type=F32)
+        t = t.reshape(4, 4, 16, 256)
+        for i in range(2):
+            g = PAIRS[2 * half + i]
+            lanes = slice(i * 128, (i + 1) * 128)
+            BASE[half, :, :, :, lanes] = t[:, :, :, lanes] + wide(H0, g)
+
+
+    base(0)
     base(1)
 
-    def finish(half, copies, got):
+    def finish(half, start, count, copies, got):
         ahead, back = copies
+        layers = slice(start, start + count)
 
         @pl.when(be)
         def _():
@@ -387,24 +399,27 @@
             p, q = fprior[0, b], flater[0, b]
             x = jnp.where(p >= 0, got[0, jnp.maximum(p, 0)].astype(F32), 0.0).astype(BF16)
             y = jnp.where(q >= 0, got[1, jnp.maximum(q, 0)].astype(F32), 0.0).astype(BF16)
-            lhs.append(jnp.concatenate([x.reshape(64, 256), y.reshape(64, 256)], axis=1))
+            lhs.append(jnp.concatenate([x.reshape(-1, 256), y.reshape(-1, 256)], axis=1))
         wt = jnp.concatenate([WT[0], WT[2]], axis=0)
         t = jnp.dot(jnp.concatenate(lhs, axis=0), wt, preferred_element_type=F32)
-        t = t.reshape(4, 4, 16, 256)
+        t = t.reshape(4, count, 16, 256)
         for i in range(2):
             g = PAIRS[2 * half + i]
             lanes = slice(i * 128, (i + 1) * 128)
-            x = (BASE[half, :, :, :, lanes] + t[:, :, :, lanes]) * wide(M, g)
-            out[0, :, :, :, g * 128 : (g + 1) * 128] = x.reshape(4, 8, 8, 128).astype(BF16)
-
-    finish(0, early, rE)
-    finish(1, late, rL)
+            mask = M[:, layers, :, g].reshape(4, count, 16, 128)
+            x = (BASE[half, :, layers, :, lanes] + t[:, :, :, lanes]) * mask
+            x = x.reshape(4, 2 * count, 8, 128).astype(BF16)
+            out[0, :, 2 * start : 2 * (start + count), :, g * 128 : (g + 1) * 128] = x
+
+    finish(0, 0, 4, early, rE)
+    for n in range(2):
+        finish(1, 2 * n, 2, late[n], rL[n])
 
     for there, copies in (
         (hi, (upward,)),
         (lo, (downward,)),
-        (af, (early[0], late[0])),
-        (be, (early[1], late[1])),
+        (af, (early[0], late[0][0], late[1][0])),
+        (be, (early[1], late[0][1], late[1][1])),
     ):
 
         @pl.when(there)
@@ -418,6 +433,7 @@
     hbm = pl.BlockSpec(memory_space=pltpu.HBM)
     left = (2, 3, 4, 5, 32, 256)
     parcels = (2, 3, 4, 16, 256)
+    halves = (2, 2, 3, 2, 16, 256)
     return pl.pallas_call(
         kernel,
         out_shape=pltpu.VMEM((1, 4, 8, 8, 512), BF16),
@@ -442,7 +458,8 @@
             pltpu.VMEM(left, BF16),
             pltpu.VMEM(left, BF16),
             pltpu.VMEM((2, 3, 1, 5, 32, 256), BF16),
-            pltpu.VMEM((2, 3072, 256), BF16),
+            pltpu.VMEM((3072, 256), BF16),
+            pltpu.VMEM((3072, 256), BF16),
             pltpu.VMEM((3, 256, 256), BF16),
             pltpu.VMEM((2, 4, 2, 8, 128), F32),
             pltpu.VMEM((2, 4, 2, 8, 128), F32),
@@ -450,13 +467,15 @@
             pltpu.VMEM((2, 13, 16, 128), BF16),
             pltpu.VMEM(parcels, BF16),
             pltpu.VMEM(parcels, BF16),
-            pltpu.VMEM(parcels, BF16),
-            pltpu.VMEM(parcels, BF16),
+            pltpu.VMEM(halves, BF16),
+            pltpu.VMEM(halves[1:], BF16),
+            pltpu.VMEM(halves[1:], BF16),
             pltpu.VMEM((2, 4, 4, 16, 256), BF16),
             pltpu.VMEM((2, 4, 4, 16, 256), F32),
             pltpu.SemaphoreType.DMA((11,)),
         ]
-        + [pltpu.SemaphoreType.DMA((2,))] * 6,
+        + [pltpu.SemaphoreType.DMA((2,))] * 4
+        + [pltpu.SemaphoreType.DMA((2, 2))] * 2,
         compiler_params=pltpu.CompilerParams(
             collective_id=0, has_side_effects=True, vmem_limit_bytes=56 << 20
         ),

time: 15.2 us -> 14.5 us (0.954)
  Pallas kernels: 14.4 us -> 13.6 us
    pallas_call x1, Pallas kernels: 14.4 us -> 13.6 us  [per_device(): pl.pallas_call(kernel, out_shape=pltpu.VMEM((1, 4, 8, 8, 512), BF16), in_...]
where the time goes in v3:
time: 14.5 us; the launch traced here: 14.3 us
  Pallas kernels  13.6 us (94%)
  local copies, waits for them, and re-layouts  0.71 us (5%)
    pallas_call x1, Pallas kernels, per_device(): pl.pallas_call(kernel, out_shape=pltpu.VMEM((1, 4, 8, 8, 512), BF16), in_...  13.6 us
    unnamed x1, local copies, waits for them, and re-layouts  0.71 us

profile of v3, /device:TPU:120, one launch (start us, length us, event | category | flops | bytes accessed | tf_op | source)
XLA Modules:
  0.0 14.3 jit_solution(234854513342628614)
XLA Ops:
  0.0 13.6 %shard_map.109 = bf16[1,4,8,8,512]{4,3,2,1,0:T(8,128)(2,1)S(1)} custom-call(bf16[1,4,8,8,512]{4,3,2,1,0:T(8,128)(2,1)} %feats.1, s32[1,4,512]{2,1,0:T(4,128)} %occ.1, bf16[2,27,64,64]{3,2,1,0:T(8,128)(2,1)} %wsp.1, f32[2,64]{1,0:T(2,128)} %bsp.1, bf16[3,64,64]{2,1,0:T(8,128)(2,1)} %wtm.1, s32[1,2]{1,0:T(1,128)} %fsend_h.1, s32[1,4,6]{2,1,0:T(4,128)} %fsrc_h.1, ...), custom_call_target="tpu_custom_call" | custom-call | tf_op jit(solution)/shard_map/pallas_call | solution.py:437
  13.6 0.7 %copy.13 = bf16[1,4,8,8,512]{4,3,2,1,0:T(8,128)(2,1)} copy(bf16[1,4,8,8,512]{4,3,2,1,0:T(8,128)(2,1)S(1)} %shard_map.109) | data formatting | bytes 524288

commit v4 on v3

--- a/solution.py
+++ b/solution.py
@@ -314,13 +314,14 @@
         beyond = jnp.where(e[:, 3:4, :] > 0.5, own[k], b)
         V.append((three(a, e, e, row), three(beyond, 0.0, 0.0, row), three(z, 0.0, 0.0, row)))
     zero = jnp.zeros((8, 8, 128), F32)
+    plain = [three(got[k][0], 0.0, 0.0, row) for k in range(2)]
     thin = jnp.zeros((16, 128), BF16)
     for dy in range(3):
         put_layers(SV, dy, 0, INNER, slice(0, 128), pair(V[0][0][dy], V[1][0][dy]))
         put_layers(SV, dy, 0, INNER, slice(128, 256), pair(V[0][1][dy], V[1][1][dy]))
         put_layers(SV, dy, 0, OUTER, slice(0, 128), pair(zero, zero))
-        x0 = jnp.where(left, 0.0, three(got[0][0], 0.0, 0.0, row)[dy])
-        x1 = jnp.where(left, three(got[1][0], 0.0, 0.0, row)[dy], 0.0)
+        x0 = jnp.where(left, 0.0, plain[0][dy])
+        x1 = jnp.where(left, plain[1][dy], 0.0)
         put_layers(SV, dy, 0, OUTER, slice(128, 256), pair(x0, x1))
         for z, at in ((0, (0, 0)), (1, (1, 4))):
             SV[at[0], dy, 0, at[1], INNER, 0:128] = pair(V[0][2][dy][z], V[1][2][dy][z])
@@ -397,8 +398,8 @@
         lhs = []
         for b in range(4):
             p, q = fprior[0, b], flater[0, b]
-            x = jnp.where(p >= 0, got[0, jnp.maximum(p, 0)].astype(F32), 0.0).astype(BF16)
-            y = jnp.where(q >= 0, got[1, jnp.maximum(q, 0)].astype(F32), 0.0).astype(BF16)
+            x = jnp.where(p >= 0, got[0, jnp.maximum(p, 0)], jnp.zeros((), BF16))
+            y = jnp.where(q >= 0, got[1, jnp.maximum(q, 0)], jnp.zeros((), BF16))
             lhs.append(jnp.concatenate([x.reshape(-1, 256), y.reshape(-1, 256)], axis=1))
         wt = jnp.concatenate([WT[0], WT[2]], axis=0)
         t = jnp.dot(jnp.concatenate(lhs, axis=0), wt, preferred_element_type=F32)

time: 14.5 us -> 14.5 us (level)
  no operation moved by 1% of the time
where the time goes in v4:
time: 14.5 us; the launch traced here: 14.3 us
  Pallas kernels  13.6 us (94%)
  local copies, waits for them, and re-layouts  0.71 us (5%)
    pallas_call x1, Pallas kernels, per_device(): pl.pallas_call(kernel, out_shape=pltpu.VMEM((1, 4, 8, 8, 512), BF16), in_...  13.6 us
    unnamed x1, local copies, waits for them, and re-layouts  0.71 us

profile of v4, /device:TPU:120, one launch (start us, length us, event | category | flops | bytes accessed | tf_op | source)
XLA Modules:
  0.0 14.3 jit_solution(11491007033388434842)
XLA Ops:
  0.0 13.6 %shard_map.109 = bf16[1,4,8,8,512]{4,3,2,1,0:T(8,128)(2,1)S(1)} custom-call(bf16[1,4,8,8,512]{4,3,2,1,0:T(8,128)(2,1)} %feats.1, s32[1,4,512]{2,1,0:T(4,128)} %occ.1, bf16[2,27,64,64]{3,2,1,0:T(8,128)(2,1)} %wsp.1, f32[2,64]{1,0:T(2,128)} %bsp.1, bf16[3,64,64]{2,1,0:T(8,128)(2,1)} %wtm.1, s32[1,2]{1,0:T(1,128)} %fsend_h.1, s32[1,4,6]{2,1,0:T(4,128)} %fsrc_h.1, ...), custom_call_target="tpu_custom_call" | custom-call | tf_op jit(solution)/shard_map/pallas_call | solution.py:438
  13.6 0.7 %copy.13 = bf16[1,4,8,8,512]{4,3,2,1,0:T(8,128)(2,1)} copy(bf16[1,4,8,8,512]{4,3,2,1,0:T(8,128)(2,1)S(1)} %shard_map.109) | data formatting | bytes 524288
